TPU v7x, 256 devices: a whole 4x4x8 slice. The times are simulated.
256 devices in a mesh: clip: 32 (over x, z_lo, y), seq: 8 (over z_hi, core).
Axes of the slice: x: 4, y: 4, z: 8 (z_hi: 4, z_lo: 2; z = z_hi * 2 + z_lo), core: 2. Of those that a mesh axis runs over, the one named last changes fastest.
Arguments:
- queries: bfloat16 [49152, 3072], P(('clip', 'seq')), parts along dimension 0, may hold values from -9 to 9
- key_heads: bfloat16 [49152, 3072], P(('clip', 'seq')), parts along dimension 0, may hold values from -9 to 9
- value_heads: bfloat16 [49152, 3072], P(('clip', 'seq')), parts along dimension 0, may hold values from -6 to 6
- query_dot: bfloat16 [49152, 3072], P(('clip', 'seq')), parts along dimension 0, may hold values from -6 to 6
- key_dot: bfloat16 [49152, 3072], P(('clip', 'seq')), parts along dimension 0, may hold values from -6 to 6
- value_dot: bfloat16 [49152, 3072], P(('clip', 'seq')), parts along dimension 0, may hold values from -6 to 6
Outputs:
- attended: bfloat16 [49152, 3072], P(('clip', 'seq')), parts along dimension 0
- attended_dot: bfloat16 [49152, 3072], P(('clip', 'seq')), parts along dimension 0
There are 32 independent parts, one for each index of `clip`. A program takes and returns all parts, laid end to end along the dimension named above; each array names one. Nothing has to cross between parts.
All inputs are finite; a program needn't handle non-finite values.
Results may differ from a plain program's by a relative error of at most 0.039.
Values may be sent and summed in bfloat16 or wider, within the bound.
A program may use at most 128 MiB of HBM per device.

v0:
```python
import jax
import jax.numpy as jnp
from jax import lax
from jax.sharding import PartitionSpec as P

E = 128


def attend_block(query_blk, qtan_blk, key_rows, value_rows, key_tan, value_tan, factor):
    scores = (
        jnp.einsum("qhe,khe->hqk", query_blk, key_rows, preferred_element_type=jnp.float32) * factor
    )
    scores_dot = (
        jnp.einsum("qhe,khe->hqk", qtan_blk, key_rows, preferred_element_type=jnp.float32)
        + jnp.einsum("qhe,khe->hqk", query_blk, key_tan, preferred_element_type=jnp.float32)
    ) * factor
    highest = jnp.max(scores, axis=2, keepdims=True)
    expd = jnp.exp(scores - highest)
    weights = expd / jnp.sum(expd, axis=2, keepdims=True)
    weights_low = weights.astype(jnp.bfloat16)
    centre = jnp.sum(weights * scores_dot, axis=2, keepdims=True)
    weights_dot = (weights * (scores_dot - centre)).astype(jnp.bfloat16)
    attended = jnp.einsum(
        "hqk,khe->qhe", weights_low, value_rows, preferred_element_type=jnp.float32
    )
    attended_dot = jnp.einsum(
        "hqk,khe->qhe", weights_dot, value_rows, preferred_element_type=jnp.float32
    ) + jnp.einsum("hqk,khe->qhe", weights_low, value_tan, preferred_element_type=jnp.float32)
    return (attended.astype(jnp.bfloat16), attended_dot.astype(jnp.bfloat16))


def full_attention(six, factor):
    query_rows, key_rows, value_rows, query_tan, key_tan, value_tan = six
    length, local_heads, head_size = query_rows.shape
    block = 512
    count = length // block

    def one_block(pair):
        return attend_block(pair[0], pair[1], key_rows, value_rows, key_tan, value_tan, factor)

    result = lax.map(
        one_block,
        (
            query_rows.reshape(count, block, local_heads, head_size),
            query_tan.reshape(count, block, local_heads, head_size),
        ),
    )
    return (
        result[0].reshape(length, local_heads, head_size),
        result[1].reshape(length, local_heads, head_size),
    )


def per_device(queries, key_heads, value_heads, query_dot, key_dot, value_dot):
    tokens = queries.shape[0]
    width = queries.shape[1]
    head_size = E
    heads_all = width // head_size
    factor = head_size ** (-0.5)
    cubes = tuple(
        (
            arr.reshape(tokens, heads_all, head_size)
            for arr in (queries, key_heads, value_heads, query_dot, key_dot, value_dot)
        )
    )
    primal = (
        lax.all_to_all(cubes[0], "seq", split_axis=1, concat_axis=0, tiled=True),
        lax.all_to_all(cubes[1], "seq", split_axis=1, concat_axis=0, tiled=True),
        lax.all_to_all(cubes[2], "seq", split_axis=1, concat_axis=0, tiled=True),
    )
    tangent = (
        lax.all_to_all(cubes[3], "seq", split_axis=1, concat_axis=0, tiled=True),
        lax.all_to_all(cubes[4], "seq", split_axis=1, concat_axis=0, tiled=True),
        lax.all_to_all(cubes[5], "seq", split_axis=1, concat_axis=0, tiled=True),
    )
    six = tuple(primal) + tuple(tangent)
    outputs = full_attention(six, factor)
    back = (
        lax.all_to_all(outputs[0], "seq", split_axis=0, concat_axis=1, tiled=True),
        lax.all_to_all(outputs[1], "seq", split_axis=0, concat_axis=1, tiled=True),
    )
    return (back[0].reshape(tokens, width), back[1].reshape(tokens, width))


def solution(mesh):
    in_specs = (
        P(("clip", "seq"), None),
        P(("clip", "seq"), None),
        P(("clip", "seq"), None),
        P(("clip", "seq"), None),
        P(("clip", "seq"), None),
        P(("clip", "seq"), None),
    )
    out_specs = (P(("clip", "seq"), None), P(("clip", "seq"), None))
    return jax.shard_map(
        per_device, mesh=mesh, in_specs=in_specs, out_specs=out_specs, check_vma=False
    )
```

profile of v0, /device:TPU:33, one launch (start us, length us, event | category | flops | bytes accessed | tf_op | source)
XLA Modules:
  0.0 433.7 jit_solution(13302937789323734484)
XLA Ops:
  0.6 0.0 copy-start
  0.6 1.3 copy-done
  1.9 1.3 copy_bitcast_fusion.4
  3.2 8.4 %all-to-all-start.1 = ((bf16[192,24,128]{2,0,1:T(8,128)(2,1)}), bf16[192,24,128]{2,0,1:T(8,128)(2,1)S(1)}, u32[]{:S(2)}, u32[]{:S(2)}) async-start(bf16[192,24,128]{2,0,1:T(8,128)(2,1)} %copy_bitcast_fusion.4), calls=%async_computation.1 | async-start | bytes 2359296 | tf_op jit(solution)/shard_map/all_to_all | solution.py:68
  11.6 0.0 copy-done.6
  11.6 1.3 copy_bitcast_fusion.3
  12.9 30.0 %all-to-all-done.1 = bf16[192,24,128]{2,0,1:T(8,128)(2,1)S(1)} async-done(((bf16[192,24,128]{2,0,1:T(8,128)(2,1)}), bf16[192,24,128]{2,0,1:T(8,128)(2,1)S(1)}, u32[]{:S(2)}, u32[]{:S(2)}) %all-to-all-start.1) | async-done | bytes 1179680 | tf_op jit(solution)/shard_map/all_to_all | solution.py:68
  43.0 4.2 all-to-all-start.2
  47.1 0.0 copy-done.7
  47.1 1.3 copy_bitcast_fusion.2
  48.5 29.4 %all-to-all-done.2 = bf16[192,24,128]{2,0,1:T(8,128)(2,1)S(1)} async-done(((bf16[192,24,128]{2,0,1:T(8,128)(2,1)}), bf16[192,24,128]{2,0,1:T(8,128)(2,1)S(1)}, u32[]{:S(2)}, u32[]{:S(2)}) %all-to-all-start.2) | async-done | bytes 1179680 | tf_op jit(solution)/shard_map/all_to_all | solution.py:69
  77.8 4.9 %all-to-all-start.3 = ((bf16[192,24,128]{2,0,1:T(8,128)(2,1)}), bf16[192,24,128]{2,0,1:T(8,128)(2,1)S(1)}, u32[]{:S(2)}, u32[]{:S(2)}) async-start(bf16[192,24,128]{2,0,1:T(8,128)(2,1)} %copy_bitcast_fusion.2), calls=%async_computation.3 | async-start | bytes 2359296 | tf_op jit(solution)/shard_map/all_to_all | solution.py:72
  82.8 2.6 copy_bitcast_fusion.1
  85.4 28.8 %all-to-all-done.3 = bf16[192,24,128]{2,0,1:T(8,128)(2,1)S(1)} async-done(((bf16[192,24,128]{2,0,1:T(8,128)(2,1)}), bf16[192,24,128]{2,0,1:T(8,128)(2,1)S(1)}, u32[]{:S(2)}, u32[]{:S(2)}) %all-to-all-start.3) | async-done | bytes 1179680 | tf_op jit(solution)/shard_map/all_to_all | solution.py:72
  114.2 1.0 copy-done.2
  115.2 4.9 %all-to-all-start.4 = ((bf16[192,24,128]{2,0,1:T(8,128)(2,1)}), bf16[192,24,128]{2,0,1:T(8,128)(2,1)}, u32[]{:S(2)}, u32[]{:S(2)}) async-start(bf16[192,24,128]{2,0,1:T(8,128)(2,1)} %copy_bitcast_fusion.1), calls=%async_computation.4 | async-start | bytes 2359296 | tf_op jit(solution)/shard_map/all_to_all | solution.py:73
  120.1 2.6 copy_bitcast_fusion
  122.7 28.2 %all-to-all-done.4 = bf16[192,24,128]{2,0,1:T(8,128)(2,1)} async-done(((bf16[192,24,128]{2,0,1:T(8,128)(2,1)}), bf16[192,24,128]{2,0,1:T(8,128)(2,1)}, u32[]{:S(2)}, u32[]{:S(2)}) %all-to-all-start.4) | async-done | bytes 1179680 | tf_op jit(solution)/shard_map/all_to_all | solution.py:73
  150.9 4.9 %all-to-all-start.5 = ((bf16[192,24,128]{2,0,1:T(8,128)(2,1)}), bf16[192,24,128]{2,0,1:T(8,128)(2,1)S(1)}, u32[]{:S(2)}, u32[]{:S(2)}) async-start(bf16[192,24,128]{2,0,1:T(8,128)(2,1)} %copy_bitcast_fusion), calls=%async_computation.5 | async-start | bytes 2359296 | tf_op jit(solution)/shard_map/all_to_all | solution.py:74
  155.8 2.6 copy_bitcast_fusion.5
  158.4 28.8 %all-to-all-done.5 = bf16[192,24,128]{2,0,1:T(8,128)(2,1)S(1)} async-done(((bf16[192,24,128]{2,0,1:T(8,128)(2,1)}), bf16[192,24,128]{2,0,1:T(8,128)(2,1)S(1)}, u32[]{:S(2)}, u32[]{:S(2)}) %all-to-all-start.5) | async-done | bytes 1179680 | tf_op jit(solution)/shard_map/all_to_all | solution.py:74
  187.2 1.0 copy-done.4
  188.2 4.9 %all-to-all-start = ((bf16[192,24,128]{2,0,1:T(8,128)(2,1)}), bf16[192,24,128]{2,0,1:T(8,128)(2,1)}, u32[]{:S(2)}, u32[]{:S(2)}) async-start(bf16[192,24,128]{2,0,1:T(8,128)(2,1)} %copy_bitcast_fusion.5), calls=%async_computation | async-start | bytes 2359296 | tf_op jit(solution)/shard_map/all_to_all | solution.py:67
  193.1 0.1 copy.37
  193.2 0.0 copy-start.3
  193.2 1.1 copy.39
  194.3 0.6 copy-done.3
  194.9 0.1 copy.41
  195.0 2.5 copy.43
  197.4 1.1 copy.45
  198.5 25.4 %all-to-all-done = bf16[192,24,128]{2,0,1:T(8,128)(2,1)} async-done(((bf16[192,24,128]{2,0,1:T(8,128)(2,1)}), bf16[192,24,128]{2,0,1:T(8,128)(2,1)}, u32[]{:S(2)}, u32[]{:S(2)}) %all-to-all-start) | async-done | bytes 1179680 | tf_op jit(solution)/shard_map/all_to_all | solution.py:67
  223.9 2.5 copy.35
  226.5 106.9 %while.12 = (s32[]{:T(128)}, bf16[3,512,3,128]{3,1,0,2:T(8,128)(2,1)}, bf16[3,512,3,128]{3,1,0,2:T(8,128)(2,1)}, bf16[3,512,3,128]{3,1,0,2:T(8,128)(2,1)}, bf16[...) while((s32[]{:T(128)}, ...), condition=%wide.region_4.5_spmd, body=%wide.region_0.4_spmd.sunk | while | flops 3662217216 | bytes 105033888 | solution.py:41
  226.5 7.5 %fusion.100 = (f32[3,512]{1,0:T(4,128)S(1)}, f32[3,512,1536]{2,1,0:T(8,128)}) fusion(bf16[1536,3,128]{2,0,1:T(8,128)(2,1)S(1)} %get-tuple-element.188, bf16[3,512,3,128]{3,1,0,2:T(8,128)(2,1)} %get-tuple-element.187, s32[]{:T(128)} %get-tuple-element.174), kind=kOutput, calls=%fused_computation.44.clone.1 | convolution fusion | flops 611059200 | bytes 11016704 | tf_op jit(solution)/shard_map/while/body/eval_jaxpr/sub | solution.py:18
  234.0 1.4 fusion.102
  235.4 7.4 %multiply_reduce_fusion.3 = (f32[3,512]{1,0:T(4,128)S(1)}, f32[3,512,1536]{2,1,0:T(8,128)}) fusion(f32[3,512,1536]{2,1,0:T(8,128)} %get-tuple-element.160, f32[3,512]{1,0:T(4,128)S(1)} %get-tuple-element.161, f32[3,512,1536]{2,1,0:T(8,128)S(1)} %fusion.102, bf16[1536,3,128]{2,0,1:T(8,128)(2,1)S(1)} %copy-done.9, ...), kind=kOutput, calls=%fused_computation.2.clone.1 | convolution fusion | flops 615774720 | bytes 29897216 | tf_op jit(solution)/shard_map/while/body/eval_jaxpr/qhe,khe->hqk/dot_general | solution.py:15
  242.8 7.5 %fusion.103 = f32[3,512,128]{2,1,0:T(8,128)S(1)} fusion(bf16[1536,3,128]{2,0,1:T(8,128)(2,1)S(1)} %get-tuple-element.189, f32[3,512,1536]{2,1,0:T(8,128)} %get-tuple-element.162, f32[3,512]{1,0:T(4,128)S(1)} %get-tuple-element.163, f32[3,512,1536]{2,1,0:T(8,128)} %get-tuple-element.160, f32[3,512]{1,0:T(4,128)S(1)} %get-tuple-element.161), kind=kOutput, calls=%fused_computation.7.clone.1 | convolution fusion | flops 613416960 | bytes 20852736 | tf_op jit(solution)/shard_map/while/body/eval_jaxpr/hqk,khe->qhe/dot_general | solution.py:26
  250.3 5.9 %fusion.104 = bf16[3,512,3,128]{3,1,0,2:T(8,128)(2,1)} fusion(bf16[3,512,3,128]{3,1,0,2:T(8,128)(2,1)} %get-tuple-element.176, s32[]{:T(128)} %get-tuple-element.174, f32[3,512,128]{2,1,0:T(8,128)S(1)} %fusion.103, bf16[1536,3,128]{2,0,1:T(8,128)(2,1)S(1)} %copy-done.10, f32[3,512,1536]{2,1,0:T(8,128)} %get-tuple-element.160, ...), kind=kOutput, calls=%fused_computation.21.clone.1 | convolution fusion | flops 609091584 | bytes 11803136 | tf_op jit(solution)/shard_map/while/body/eval_jaxpr/hqk,khe->qhe/dot_general | solution.py:28
  256.3 5.9 %fusion.101 = bf16[3,512,3,128]{3,1,0,2:T(8,128)(2,1)} fusion(bf16[3,512,3,128]{3,1,0,2:T(8,128)(2,1)} %get-tuple-element.175, s32[]{:T(128)} %get-tuple-element.174, bf16[1536,3,128]{2,0,1:T(8,128)(2,1)S(1)} %get-tuple-element.189, f32[3,512,1536]{2,1,0:T(8,128)} %get-tuple-element.160, f32[3,512]{1,0:T(4,128)S(1)} %get-tuple-element.161), kind=kOutput, calls=%fused_computation.19.clone.1 | convolution fusion | flops 608894976 | bytes 11016704 | tf_op jit(solution)/shard_map/while/body/eval_jaxpr/hqk,khe->qhe/dot_general | solution.py:23
  262.1 7.5 %fusion.100 = (f32[3,512]{1,0:T(4,128)S(1)}, f32[3,512,1536]{2,1,0:T(8,128)}) fusion(bf16[1536,3,128]{2,0,1:T(8,128)(2,1)S(1)} %get-tuple-element.188, bf16[3,512,3,128]{3,1,0,2:T(8,128)(2,1)} %get-tuple-element.187, s32[]{:T(128)} %get-tuple-element.174), kind=kOutput, calls=%fused_computation.44.clone.1 | convolution fusion | flops 611059200 | bytes 11016704 | tf_op jit(solution)/shard_map/while/body/eval_jaxpr/sub | solution.py:18
  269.6 1.4 fusion.102
  271.0 7.4 %multiply_reduce_fusion.3 = (f32[3,512]{1,0:T(4,128)S(1)}, f32[3,512,1536]{2,1,0:T(8,128)}) fusion(f32[3,512,1536]{2,1,0:T(8,128)} %get-tuple-element.160, f32[3,512]{1,0:T(4,128)S(1)} %get-tuple-element.161, f32[3,512,1536]{2,1,0:T(8,128)S(1)} %fusion.102, bf16[1536,3,128]{2,0,1:T(8,128)(2,1)S(1)} %copy-done.9, ...), kind=kOutput, calls=%fused_computation.2.clone.1 | convolution fusion | flops 615774720 | bytes 29897216 | tf_op jit(solution)/shard_map/while/body/eval_jaxpr/qhe,khe->hqk/dot_general | solution.py:15
  278.4 7.5 %fusion.103 = f32[3,512,128]{2,1,0:T(8,128)S(1)} fusion(bf16[1536,3,128]{2,0,1:T(8,128)(2,1)S(1)} %get-tuple-element.189, f32[3,512,1536]{2,1,0:T(8,128)} %get-tuple-element.162, f32[3,512]{1,0:T(4,128)S(1)} %get-tuple-element.163, f32[3,512,1536]{2,1,0:T(8,128)} %get-tuple-element.160, f32[3,512]{1,0:T(4,128)S(1)} %get-tuple-element.161), kind=kOutput, calls=%fused_computation.7.clone.1 | convolution fusion | flops 613416960 | bytes 20852736 | tf_op jit(solution)/shard_map/while/body/eval_jaxpr/hqk,khe->qhe/dot_general | solution.py:26
  286.0 5.9 %fusion.104 = bf16[3,512,3,128]{3,1,0,2:T(8,128)(2,1)} fusion(bf16[3,512,3,128]{3,1,0,2:T(8,128)(2,1)} %get-tuple-element.176, s32[]{:T(128)} %get-tuple-element.174, f32[3,512,128]{2,1,0:T(8,128)S(1)} %fusion.103, bf16[1536,3,128]{2,0,1:T(8,128)(2,1)S(1)} %copy-done.10, f32[3,512,1536]{2,1,0:T(8,128)} %get-tuple-element.160, ...), kind=kOutput, calls=%fused_computation.21.clone.1 | convolution fusion | flops 609091584 | bytes 11803136 | tf_op jit(solution)/shard_map/while/body/eval_jaxpr/hqk,khe->qhe/dot_general | solution.py:28
  291.9 5.9 %fusion.101 = bf16[3,512,3,128]{3,1,0,2:T(8,128)(2,1)} fusion(bf16[3,512,3,128]{3,1,0,2:T(8,128)(2,1)} %get-tuple-element.175, s32[]{:T(128)} %get-tuple-element.174, bf16[1536,3,128]{2,0,1:T(8,128)(2,1)S(1)} %get-tuple-element.189, f32[3,512,1536]{2,1,0:T(8,128)} %get-tuple-element.160, f32[3,512]{1,0:T(4,128)S(1)} %get-tuple-element.161), kind=kOutput, calls=%fused_computation.19.clone.1 | convolution fusion | flops 608894976 | bytes 11016704 | tf_op jit(solution)/shard_map/while/body/eval_jaxpr/hqk,khe->qhe/dot_general | solution.py:23
  297.7 7.5 %fusion.100 = (f32[3,512]{1,0:T(4,128)S(1)}, f32[3,512,1536]{2,1,0:T(8,128)}) fusion(bf16[1536,3,128]{2,0,1:T(8,128)(2,1)S(1)} %get-tuple-element.188, bf16[3,512,3,128]{3,1,0,2:T(8,128)(2,1)} %get-tuple-element.187, s32[]{:T(128)} %get-tuple-element.174), kind=kOutput, calls=%fused_computation.44.clone.1 | convolution fusion | flops 611059200 | bytes 11016704 | tf_op jit(solution)/shard_map/while/body/eval_jaxpr/sub | solution.py:18
  305.2 1.4 fusion.102
  306.6 7.4 %multiply_reduce_fusion.3 = (f32[3,512]{1,0:T(4,128)S(1)}, f32[3,512,1536]{2,1,0:T(8,128)}) fusion(f32[3,512,1536]{2,1,0:T(8,128)} %get-tuple-element.160, f32[3,512]{1,0:T(4,128)S(1)} %get-tuple-element.161, f32[3,512,1536]{2,1,0:T(8,128)S(1)} %fusion.102, bf16[1536,3,128]{2,0,1:T(8,128)(2,1)S(1)} %copy-done.9, ...), kind=kOutput, calls=%fused_computation.2.clone.1 | convolution fusion | flops 615774720 | bytes 29897216 | tf_op jit(solution)/shard_map/while/body/eval_jaxpr/qhe,khe->hqk/dot_general | solution.py:15
  314.1 7.5 %fusion.103 = f32[3,512,128]{2,1,0:T(8,128)S(1)} fusion(bf16[1536,3,128]{2,0,1:T(8,128)(2,1)S(1)} %get-tuple-element.189, f32[3,512,1536]{2,1,0:T(8,128)} %get-tuple-element.162, f32[3,512]{1,0:T(4,128)S(1)} %get-tuple-element.163, f32[3,512,1536]{2,1,0:T(8,128)} %get-tuple-element.160, f32[3,512]{1,0:T(4,128)S(1)} %get-tuple-element.161), kind=kOutput, calls=%fused_computation.7.clone.1 | convolution fusion | flops 613416960 | bytes 20852736 | tf_op jit(solution)/shard_map/while/body/eval_jaxpr/hqk,khe->qhe/dot_general | solution.py:26
  321.6 5.9 %fusion.104 = bf16[3,512,3,128]{3,1,0,2:T(8,128)(2,1)} fusion(bf16[3,512,3,128]{3,1,0,2:T(8,128)(2,1)} %get-tuple-element.176, s32[]{:T(128)} %get-tuple-element.174, f32[3,512,128]{2,1,0:T(8,128)S(1)} %fusion.103, bf16[1536,3,128]{2,0,1:T(8,128)(2,1)S(1)} %copy-done.10, f32[3,512,1536]{2,1,0:T(8,128)} %get-tuple-element.160, ...), kind=kOutput, calls=%fused_computation.21.clone.1 | convolution fusion | flops 609091584 | bytes 11803136 | tf_op jit(solution)/shard_map/while/body/eval_jaxpr/hqk,khe->qhe/dot_general | solution.py:28
  327.5 5.9 %fusion.101 = bf16[3,512,3,128]{3,1,0,2:T(8,128)(2,1)} fusion(bf16[3,512,3,128]{3,1,0,2:T(8,128)(2,1)} %get-tuple-element.175, s32[]{:T(128)} %get-tuple-element.174, bf16[1536,3,128]{2,0,1:T(8,128)(2,1)S(1)} %get-tuple-element.189, f32[3,512,1536]{2,1,0:T(8,128)} %get-tuple-element.160, f32[3,512]{1,0:T(4,128)S(1)} %get-tuple-element.161), kind=kOutput, calls=%fused_computation.19.clone.1 | convolution fusion | flops 608894976 | bytes 11016704 | tf_op jit(solution)/shard_map/while/body/eval_jaxpr/hqk,khe->qhe/dot_general | solution.py:23
  333.4 8.1 %copy.49 = bf16[1536,3,128]{2,1,0:T(4,128)(2,1)} copy(bf16[1536,3,128]{2,0,1:T(8,128)(2,1)} %bitcast.24) | data formatting | bytes 2359296 | tf_op jit(solution)/shard_map/reshape | solution.py:49
  341.5 5.0 %all-to-all-start.6 = ((bf16[1536,3,128]{2,1,0:T(4,128)(2,1)}), bf16[1536,3,128]{2,1,0:T(4,128)(2,1)S(1)}, u32[]{:S(2)}, u32[]{:S(2)}) async-start(bf16[1536,3,128]{2,1,0:T(4,128)(2,1)} %copy.49), calls=%async_computation.6 | async-start | bytes 3145728 | tf_op jit(solution)/shard_map/all_to_all | solution.py:79
  346.5 8.2 %copy.53 = bf16[1536,3,128]{2,1,0:T(4,128)(2,1)} copy(bf16[1536,3,128]{2,0,1:T(8,128)(2,1)S(1)} %bitcast.143) | data formatting | bytes 2359296 | tf_op jit(solution)/shard_map/reshape | solution.py:50
  354.7 31.6 %all-to-all-done.6 = bf16[1536,3,128]{2,1,0:T(4,128)(2,1)S(1)} async-done(((bf16[1536,3,128]{2,1,0:T(4,128)(2,1)}), bf16[1536,3,128]{2,1,0:T(4,128)(2,1)S(1)}, u32[]{:S(2)}, u32[]{:S(2)}) %all-to-all-start.6) | async-done | bytes 1179680 | tf_op jit(solution)/shard_map/all_to_all | solution.py:79
  386.3 4.2 all-to-all-start.7
  390.5 0.2 copy.50
  390.7 1.0 copy.51
  391.7 2.2 reshape.56
  393.9 36.4 %all-to-all-done.7 = bf16[1536,3,128]{2,1,0:T(4,128)(2,1)S(1)} async-done(((bf16[1536,3,128]{2,1,0:T(4,128)(2,1)}), bf16[1536,3,128]{2,1,0:T(4,128)(2,1)S(1)}, u32[]{:S(2)}, u32[]{:S(2)}) %all-to-all-start.7) | async-done | bytes 1179680 | tf_op jit(solution)/shard_map/all_to_all | solution.py:80
  430.3 0.2 copy.54
  430.5 0.0 copy-start.1
  430.5 1.0 copy.55
  431.5 2.2 reshape.58
  (25 shorter events, 0.0 us)
Async XLA Ops:
  0.6 1.3 copy-start
  3.2 8.4 %copy-start.6 = (bf16[192,3072]{1,0:T(8,128)(2,1)S(1)}, bf16[192,3072]{1,0:T(8,128)(2,1)}, u32[]{:S(2)}) copy-start(bf16[192,3072]{1,0:T(8,128)(2,1)} %param.10) | copy-start | bytes 3538948
  3.2 39.7 %all-to-all-start.1 = ((bf16[192,24,128]{2,0,1:T(8,128)(2,1)}), bf16[192,24,128]{2,0,1:T(8,128)(2,1)S(1)}, u32[]{:S(2)}, u32[]{:S(2)}) async-start(bf16[192,24,128]{2,0,1:T(8,128)(2,1)} %copy_bitcast_fusion.4), calls=%async_computation.1 | async-start | bytes 2359296 | tf_op jit(solution)/shard_map/all_to_all | solution.py:68
  12.9 34.2 %copy-start.7 = (bf16[192,3072]{1,0:T(8,128)(2,1)S(1)}, bf16[192,3072]{1,0:T(8,128)(2,1)}, u32[]{:S(2)}) copy-start(bf16[192,3072]{1,0:T(8,128)(2,1)} %param.11) | copy-start | bytes 3538948
  43.0 34.9 %all-to-all-start.2 = ((bf16[192,24,128]{2,0,1:T(8,128)(2,1)}), bf16[192,24,128]{2,0,1:T(8,128)(2,1)S(1)}, u32[]{:S(2)}, u32[]{:S(2)}) async-start(bf16[192,24,128]{2,0,1:T(8,128)(2,1)} %copy_bitcast_fusion.3), calls=%async_computation.2 | async-start | bytes 2359296 | tf_op jit(solution)/shard_map/all_to_all | solution.py:69
  77.8 36.3 %all-to-all-start.3 = ((bf16[192,24,128]{2,0,1:T(8,128)(2,1)}), bf16[192,24,128]{2,0,1:T(8,128)(2,1)S(1)}, u32[]{:S(2)}, u32[]{:S(2)}) async-start(bf16[192,24,128]{2,0,1:T(8,128)(2,1)} %copy_bitcast_fusion.2), calls=%async_computation.3 | async-start | bytes 2359296 | tf_op jit(solution)/shard_map/all_to_all | solution.py:72
  114.2 1.0 copy-start.2
  115.2 35.7 %all-to-all-start.4 = ((bf16[192,24,128]{2,0,1:T(8,128)(2,1)}), bf16[192,24,128]{2,0,1:T(8,128)(2,1)}, u32[]{:S(2)}, u32[]{:S(2)}) async-start(bf16[192,24,128]{2,0,1:T(8,128)(2,1)} %copy_bitcast_fusion.1), calls=%async_computation.4 | async-start | bytes 2359296 | tf_op jit(solution)/shard_map/all_to_all | solution.py:73
  150.9 36.3 %all-to-all-start.5 = ((bf16[192,24,128]{2,0,1:T(8,128)(2,1)}), bf16[192,24,128]{2,0,1:T(8,128)(2,1)S(1)}, u32[]{:S(2)}, u32[]{:S(2)}) async-start(bf16[192,24,128]{2,0,1:T(8,128)(2,1)} %copy_bitcast_fusion), calls=%async_computation.5 | async-start | bytes 2359296 | tf_op jit(solution)/shard_map/all_to_all | solution.py:74
  187.2 1.0 copy-start.4
  188.2 35.7 %all-to-all-start = ((bf16[192,24,128]{2,0,1:T(8,128)(2,1)}), bf16[192,24,128]{2,0,1:T(8,128)(2,1)}, u32[]{:S(2)}, u32[]{:S(2)}) async-start(bf16[192,24,128]{2,0,1:T(8,128)(2,1)} %copy_bitcast_fusion.5), calls=%async_computation | async-start | bytes 2359296 | tf_op jit(solution)/shard_map/all_to_all | solution.py:67
  193.2 1.7 copy-start.3
  195.0 2.5 copy-start.5
  223.9 2.5 copy-start.8
  233.9 1.4 copy-start.9
  242.8 7.5 %copy-start.10 = (bf16[1536,3,128]{2,0,1:T(8,128)(2,1)S(1)}, bf16[1536,3,128]{2,0,1:T(8,128)(2,1)}, u32[]{:S(2)}) copy-start(bf16[1536,3,128]{2,0,1:T(8,128)(2,1)} %get-tuple-element.192) | copy-start | bytes 3538948 | tf_op jit(solution)/shard_map/while
  269.6 1.4 copy-start.9
  278.4 7.5 %copy-start.10 = (bf16[1536,3,128]{2,0,1:T(8,128)(2,1)S(1)}, bf16[1536,3,128]{2,0,1:T(8,128)(2,1)}, u32[]{:S(2)}) copy-start(bf16[1536,3,128]{2,0,1:T(8,128)(2,1)} %get-tuple-element.192) | copy-start | bytes 3538948 | tf_op jit(solution)/shard_map/while
  305.2 1.4 copy-start.9
  314.1 7.5 %copy-start.10 = (bf16[1536,3,128]{2,0,1:T(8,128)(2,1)S(1)}, bf16[1536,3,128]{2,0,1:T(8,128)(2,1)}, u32[]{:S(2)}) copy-start(bf16[1536,3,128]{2,0,1:T(8,128)(2,1)} %get-tuple-element.192) | copy-start | bytes 3538948 | tf_op jit(solution)/shard_map/while
  341.4 5.0 %copy-start.11 = (bf16[3,512,3,128]{3,1,0,2:T(8,128)(2,1)S(1)}, bf16[3,512,3,128]{3,1,0,2:T(8,128)(2,1)}, u32[]{:S(2)}) copy-start(bf16[3,512,3,128]{3,1,0,2:T(8,128)(2,1)} %get-tuple-element.51) | copy-start | bytes 3538948
  341.5 44.8 %all-to-all-start.6 = ((bf16[1536,3,128]{2,1,0:T(4,128)(2,1)}), bf16[1536,3,128]{2,1,0:T(4,128)(2,1)S(1)}, u32[]{:S(2)}, u32[]{:S(2)}) async-start(bf16[1536,3,128]{2,1,0:T(4,128)(2,1)} %copy.49), calls=%async_computation.6 | async-start | bytes 3145728 | tf_op jit(solution)/shard_map/all_to_all | solution.py:79
  386.3 44.0 %all-to-all-start.7 = ((bf16[1536,3,128]{2,1,0:T(4,128)(2,1)}), bf16[1536,3,128]{2,1,0:T(4,128)(2,1)S(1)}, u32[]{:S(2)}, u32[]{:S(2)}) async-start(bf16[1536,3,128]{2,1,0:T(4,128)(2,1)} %copy.53), calls=%async_computation.7 | async-start | bytes 3145728 | tf_op jit(solution)/shard_map/all_to_all | solution.py:80
  430.5 3.2 copy-start.1
where the time goes:
time: 436 us; the launch traced here: 434 us
  waiting for transfers between devices  239 us (55%)
  matrix products  107 us (25%)
  local copies, waits for them, and re-layouts  46.2 us (11%)
  starting transfers between devices  41.4 us (9%)
    all_to_all x1, waiting for transfers between devices, per_device(): lax.all_to_all(outputs[1], 'seq', split_axis=0, concat_axis=1, tiled=True)  36.4 us
    all_to_all x1, waiting for transfers between devices, per_device(): lax.all_to_all(outputs[0], 'seq', split_axis=0, concat_axis=1, tiled=True)  31.6 us
    all_to_all x1, waiting for transfers between devices, per_device(): lax.all_to_all(cubes[1], 'seq', split_axis=1, concat_axis=0, tiled=True)  30 us
    all_to_all x1, waiting for transfers between devices, per_device(): lax.all_to_all(cubes[2], 'seq', split_axis=1, concat_axis=0, tiled=True)  29.4 us
    all_to_all x1, waiting for transfers between devices, per_device(): lax.all_to_all(cubes[3], 'seq', split_axis=1, concat_axis=0, tiled=True)  28.8 us
    all_to_all x1, waiting for transfers between devices, per_device(): lax.all_to_all(cubes[5], 'seq', split_axis=1, concat_axis=0, tiled=True)  28.8 us
    all_to_all x1, waiting for transfers between devices, per_device(): lax.all_to_all(cubes[4], 'seq', split_axis=1, concat_axis=0, tiled=True)  28.2 us
    all_to_all x1, waiting for transfers between devices, per_device(): lax.all_to_all(cubes[0], 'seq', split_axis=1, concat_axis=0, tiled=True)  25.4 us
  transfers between devices with their start and end apart: 8, of which 8 were waited for; matrix products, arithmetic and copies ran while one was open for 6% of the time, Pallas kernels for 0%

commit v1 on v0

v1 whole, which is shorter than its diff:
```python
import functools

import jax
import jax.numpy as jnp
from jax import lax
from jax.experimental import pallas as pl
from jax.experimental.pallas import tpu as pltpu
from jax.sharding import PartitionSpec as P

E = 128
CORES = 2
MESH = pl.DeviceIdType.MESH
LOG2E = 1.4426950408889634
NT = (((1,), (1,)), ((), ()))
NN = (((1,), (0,)), ((), ()))


def attend(query, query_tan, keys, key_tan, values, value_tan):
    factor = E ** (-0.5)
    scores = lax.dot_general(query, keys, NT, preferred_element_type=jnp.float32)
    scores_dot = lax.dot_general(
        jnp.concatenate([query_tan, query], axis=1),
        jnp.concatenate([keys, key_tan], axis=1),
        NT,
        preferred_element_type=jnp.float32,
    )
    highest = jnp.max(scores, axis=1, keepdims=True)
    expd = jnp.exp2((scores - highest) * (factor * LOG2E))
    inverse = 1.0 / jnp.sum(expd, axis=1, keepdims=True)
    centre = jnp.sum(expd * scores_dot, axis=1, keepdims=True) * inverse
    expd_low = expd.astype(jnp.bfloat16)
    expd_dot = (expd * (scores_dot - centre)).astype(jnp.bfloat16)
    both = lax.dot_general(
        expd_low,
        jnp.concatenate([values, value_tan], axis=1),
        NN,
        preferred_element_type=jnp.float32,
    )
    moved = lax.dot_general(expd_dot, values, NN, preferred_element_type=jnp.float32)
    attended = both[:, :E] * inverse
    attended_dot = (moved * factor + both[:, E:]) * inverse
    return attended.astype(jnp.bfloat16), attended_dot.astype(jnp.bfloat16)


def kernel(n, heads, *refs):
    sources, results = refs[:6], refs[6:8]
    held, done = refs[8:10]
    send_in, recv_in, own_in, send_out, recv_out, own_out = refs[10:]
    tokens = sources[0].shape[0]
    chips = n // CORES
    me = lax.axis_index("seq")
    chip, core = me // CORES, lax.rem(me, CORES)

    barrier = pltpu.get_barrier_semaphore()
    for step in range(1, n):
        pl.semaphore_signal(
            barrier, inc=1, device_id={"seq": lax.rem(me + step, n)}, device_id_type=MESH
        )

    def columns(device, head):
        return pl.ds(pl.multiple_of((device * heads + head) * E, E), E)

    def rows(device):
        return pl.ds(pl.multiple_of(device * tokens, tokens), tokens)

    for head in range(heads):
        for i, source in enumerate(sources):
            pltpu.make_async_copy(
                source.at[:, columns(me, head)], held.at[head, i, rows(me)], own_in.at[head]
            ).start()
    pl.semaphore_wait(barrier, n - 1)

    def partner(order):
        over = lax.rem(order, chips)
        over = lax.rem(over + 1, chips)
        side = lax.rem(order // chips + core, CORES)
        return lax.rem(chip + over, chips) * CORES + side

    def send_head(head):
        def to_one(order, carry):
            other = partner(order)

            @pl.when(other != me)
            def _():
                for i, source in enumerate(sources):
                    pltpu.make_async_remote_copy(
                        src_ref=source.at[:, columns(other, head)],
                        dst_ref=held.at[head, i, rows(me)],
                        send_sem=send_in,
                        recv_sem=recv_in.at[head],
                        device_id={"seq": other},
                        device_id_type=MESH,
                    ).start()

            return carry

        lax.fori_loop(0, n, to_one, 0)

    def wait_for(ref, sem):
        pltpu.make_async_copy(ref, ref, sem).wait()

    far = (n - 1) * tokens
    send_head(0)
    send_head(1)

    def one_head(head, carry):
        wait_for(held.at[head, :, pl.ds(0, far)], recv_in.at[head])
        wait_for(held.at[head, :, pl.ds(0, tokens)], own_in.at[head])

        @pl.when(head < heads - 2)
        def _():
            send_head(head + 2)

        def one_chip(step, inner):
            there = lax.rem(chip + 1 + step, chips)
            block = pl.ds(
                pl.multiple_of(there * (CORES * tokens), CORES * tokens), CORES * tokens
            )
            out = attend(
                held[head, 0, block],
                held[head, 3, block],
                held[head, 1],
                held[head, 4],
                held[head, 2],
                held[head, 5],
            )
            for i in range(2):
                done[i, head, block] = out[i]
            for side in range(CORES):
                other = there * CORES + side

                @pl.when(other != me)
                def _():
                    for i in range(2):
                        pltpu.make_async_remote_copy(
                            src_ref=done.at[i, head, rows(other)],
                            dst_ref=results[i].at[:, columns(me, head)],
                            send_sem=send_out,
                            recv_sem=recv_out.at[i],
                            device_id={"seq": other},
                            device_id_type=MESH,
                        ).start()

                @pl.when(other == me)
                def _():
                    for i in range(2):
                        pltpu.make_async_copy(
                            done.at[i, head, rows(me)],
                            results[i].at[:, columns(me, head)],
                            own_out.at[i],
                        ).start()

            return inner

        lax.fori_loop(0, chips, one_chip, 0)
        return carry

    lax.fori_loop(0, heads, one_head, 0)
    wide = (n - 1) * heads * E
    for i in range(2):
        wait_for(results[i].at[:, pl.ds(0, heads * E)], own_out.at[i])
        wait_for(results[i].at[:, pl.ds(0, wide)], recv_out.at[i])
    wait_for(done.at[:, :, pl.ds(0, far)], send_out)
    wait_for(held.at[:, :, pl.ds(0, far)], send_in)


def per_device(n, *arrays):
    tokens, width = arrays[0].shape
    heads = width // E // n
    length = tokens * n
    shape = jax.ShapeDtypeStruct((tokens, width), jnp.bfloat16)
    return pl.pallas_call(
        functools.partial(kernel, n, heads),
        out_shape=(shape, shape),
        in_specs=[pl.BlockSpec(memory_space=pl.ANY)] * 6,
        out_specs=[pl.BlockSpec(memory_space=pl.ANY)] * 2,
        scratch_shapes=[
            pltpu.VMEM((heads, 6, length, E), jnp.bfloat16),
            pltpu.VMEM((2, heads, length, E), jnp.bfloat16),
            pltpu.SemaphoreType.DMA,
            pltpu.SemaphoreType.DMA((heads,)),
            pltpu.SemaphoreType.DMA((heads,)),
            pltpu.SemaphoreType.DMA,
            pltpu.SemaphoreType.DMA((2,)),
            pltpu.SemaphoreType.DMA((2,)),
        ],
        compiler_params=pltpu.CompilerParams(
            collective_id=0, has_side_effects=True, vmem_limit_bytes=56 * 1024 * 1024
        ),
    )(*arrays)


def solution(mesh):
    spec = P(("clip", "seq"), None)
    return jax.shard_map(
        functools.partial(per_device, mesh.shape["seq"]),
        mesh=mesh,
        in_specs=(spec,) * 6,
        out_specs=(spec,) * 2,
        check_vma=False,
    )
```

time: 436 us -> 218 us (0.50)
  waiting for transfers between devices: 239 us -> 0 us
  Pallas kernels: 0 us -> 211 us
  matrix products: 107 us -> 0 us
  local copies, waits for them, and re-layouts: 46.2 us -> 3.47 us
  starting transfers between devices: 41.4 us -> 0 us
    all_to_all x8 -> x0, waiting for transfers between devices: 239 us -> none  [the longest x1 36.4 us: per_device(): lax.all_to_all(outputs[1], 'seq', split_axis=0, concat_axis=1, tiled=True)]
    pallas_call x0 -> x1, Pallas kernels: none -> 211 us  [per_device(): pl.pallas_call(functools.partial(kernel, n, heads), out_shape=(shape, sha...]
    dot_general x15 -> x0, matrix products: 84.4 us -> none  [the longest x3 22.5 us: attend_block(): jnp.einsum('hqk,khe->qhe', weights_dot, value_rows, preferred_element_typ...]
    all_to_all x8 -> x0, starting transfers between devices: 41.4 us -> none  [the longest x1 8.37 us: per_device(): lax.all_to_all(cubes[1], 'seq', split_axis=1, concat_axis=0, tiled=True)]
    reshape x10 -> x0, local copies, waits for them, and re-layouts: 32.5 us -> none  [the longest x6 11.8 us: per_device(): arr.reshape(tokens, heads_all, head_size)]
    sub x3 -> x0, matrix products: 22.4 us -> none  [attend_block(): expd = jnp.exp(scores - highest)]
    all_to_all x10 -> x0, local copies, waits for them, and re-layouts: 9.76 us -> none  [the longest x1 2.53 us: per_device(): lax.all_to_all(cubes[0], 'seq', split_axis=1, concat_axis=0, tiled=True)]
  transfers between devices with their start and end apart: 8 -> 0, of which waited for: 8 -> 0; matrix products, arithmetic and copies ran while one was open for 6% -> 0% of each run, Pallas kernels for 0% -> 0%
where the time goes in v1:
time: 218 us; the launch traced here: 215 us
  Pallas kernels  211 us (97%)
  local copies, waits for them, and re-layouts  3.47 us (2%)
    pallas_call x1, Pallas kernels, per_device(): pl.pallas_call(functools.partial(kernel, n, heads), out_shape=(shape, sha...  211 us

profile of v1, /device:TPU:33, one launch (start us, length us, event | category | flops | bytes accessed | tf_op | source)
XLA Modules:
  0.0 215.2 jit_solution(8180738011122281940)
XLA Ops:
  0.6 211.1 %shard_map.77 = (bf16[192,3072]{1,0:T(8,128)(2,1)}, bf16[192,3072]{1,0:T(8,128)(2,1)}) custom-call(bf16[192,3072]{1,0:T(8,128)(2,1)} %refs_0_.1, bf16[192,3072]{1,0:T(8,128)(2,1)} %refs_1_.1, bf16[192,3072]{1,0:T(8,128)(2,1)} %refs_2_.1, bf16[192,3072]{1,0:T(8,128)(2,1)} %refs_3_.1, bf16[192,3072]{1,0:T(8,128)(2,1)} %refs_4_.1, bf16[192,3072]{1,0:T(8,128)(2,1)} %refs_5_.1), custom_call_target="tpu_custom_call" | custom-call | tf_op jit(solution)/shard_map/pallas_call | solution.py:172
  211.7 0.0 copy-start
  211.8 2.5 %copy.10 = bf16[192,3072]{1,0:T(8,128)(2,1)} copy(bf16[192,3072]{1,0:T(8,128)(2,1)} %get-tuple-element.4) | data formatting | bytes 2359296
  214.2 0.0 copy-done
  214.2 1.0 copy.11
Async XLA Ops:
  211.7 2.5 %copy-start = (bf16[192,3072]{1,0:T(8,128)(2,1)S(1)}, bf16[192,3072]{1,0:T(8,128)(2,1)}, u32[]{:S(2)}) copy-start(bf16[192,3072]{1,0:T(8,128)(2,1)} %get-tuple-element.5) | copy-start | bytes 3538948

commit v2 on v1

v2 whole, which is shorter than its diff:
```python
import functools

import jax
import jax.numpy as jnp
from jax import lax
from jax.experimental import pallas as pl
from jax.experimental.pallas import tpu as pltpu
from jax.sharding import PartitionSpec as P

E = 128
CORES = 2
MESH = pl.DeviceIdType.MESH
LOG2E = 1.4426950408889634
NT = (((1,), (1,)), ((), ()))
NN = (((1,), (0,)), ((), ()))


def attend(query, query_tan, keys, key_tan, values, value_tan):
    factor = E ** (-0.5)
    scores = lax.dot_general(query, keys, NT, preferred_element_type=jnp.float32)
    scores_dot = lax.dot_general(
        jnp.concatenate([query_tan, query], axis=1),
        jnp.concatenate([keys, key_tan], axis=1),
        NT,
        preferred_element_type=jnp.float32,
    )
    highest = jnp.max(scores, axis=1, keepdims=True)
    expd = jnp.exp2((scores - highest) * (factor * LOG2E))
    inverse = 1.0 / jnp.sum(expd, axis=1, keepdims=True)
    centre = jnp.sum(expd * scores_dot, axis=1, keepdims=True) * inverse
    expd_low = expd.astype(jnp.bfloat16)
    expd_dot = (expd * (scores_dot - centre)).astype(jnp.bfloat16)
    both = lax.dot_general(
        expd_low,
        jnp.concatenate([values, value_tan], axis=1),
        NN,
        preferred_element_type=jnp.float32,
    )
    moved = lax.dot_general(expd_dot, values, NN, preferred_element_type=jnp.float32)
    attended = both[:, :E] * inverse
    attended_dot = (moved * factor + both[:, E:]) * inverse
    return attended.astype(jnp.bfloat16), attended_dot.astype(jnp.bfloat16)


def kernel(n, heads, *refs):
    sources, results = refs[:6], refs[6:8]
    held, done = refs[8:10]
    ready, send_in, recv_in, own_in, send_out, recv_out, own_out = refs[10:]
    tokens = sources[0].shape[0]
    chips = n // CORES
    me = lax.axis_index("seq")
    chip, core = me // CORES, lax.rem(me, CORES)
    turned = lax.rem(lax.axis_index("clip") // 4, 2) == 0

    def along(place):
        return jnp.where(turned & (place >= 2), 5 - place, place)

    rank = along(chip) * CORES + (CORES - 1 - core)

    def at_rank(r):
        return along(r // CORES) * CORES + (CORES - 1 - lax.rem(r, CORES))

    def signal(semaphore, device):
        pl.semaphore_signal(
            semaphore, inc=1, device_id={"seq": device}, device_id_type=MESH
        )

    def loop(start, stop, body):
        def step(i, carry):
            body(i)
            return carry

        lax.fori_loop(start, stop, step, 0)

    def columns(device, head):
        return pl.ds(pl.multiple_of((device * heads + head) * E, E), E)

    def rows(device):
        return pl.ds(pl.multiple_of(device * tokens, tokens), tokens)

    def send(head, other):
        for i, source in enumerate(sources):
            pltpu.make_async_remote_copy(
                src_ref=source.at[:, columns(other, head)],
                dst_ref=held.at[head, i, rows(me)],
                send_sem=send_in,
                recv_sem=recv_in.at[head],
                device_id={"seq": other},
                device_id_type=MESH,
            ).start()

    def wait_for(ref, sem):
        pltpu.make_async_copy(ref, ref, sem).wait()

    barrier = pltpu.get_barrier_semaphore()
    loop(rank + 1, n, lambda r: signal(barrier, at_rank(r)))
    pl.when(rank > 0)(lambda: pl.semaphore_wait(barrier, rank))
    loop(0, rank, lambda r: signal(ready.at[me], at_rank(r)))
    loop(0, rank, lambda r: send(0, at_rank(r)))

    def greeted(r):
        pl.semaphore_wait(ready.at[at_rank(r)], 1)
        send(0, at_rank(r))

    loop(rank + 1, n, greeted)

    def own(head):
        for i, source in enumerate(sources):
            pltpu.make_async_copy(
                source.at[:, columns(me, head)], held.at[head, i, rows(me)], own_in.at[head]
            ).start()

    loop(0, heads, own)

    def partner(step):
        over = lax.rem(step // CORES + 1, chips)
        side = 1 - lax.rem(step, CORES)
        return lax.rem(chip + over, chips) * CORES + lax.rem(core + side, CORES)

    def send_head(head):
        loop(0, n - 1, lambda step: send(head, partner(step)))

    def send_out_to(head, other):
        @pl.when(other != me)
        def _():
            for i in range(2):
                pltpu.make_async_remote_copy(
                    src_ref=done.at[i, head, rows(other)],
                    dst_ref=results[i].at[:, columns(me, head)],
                    send_sem=send_out,
                    recv_sem=recv_out.at[i],
                    device_id={"seq": other},
                    device_id_type=MESH,
                ).start()

        @pl.when(other == me)
        def _():
            for i in range(2):
                pltpu.make_async_copy(
                    done.at[i, head, rows(me)],
                    results[i].at[:, columns(me, head)],
                    own_out.at[i],
                ).start()

    far = (n - 1) * tokens
    send_head(1)

    def one_head(head):
        wait_for(held.at[head, :, pl.ds(0, far)], recv_in.at[head])
        wait_for(held.at[head, :, pl.ds(0, tokens)], own_in.at[head])

        @pl.when(head < heads - 2)
        def _():
            send_head(head + 2)

        @pl.when(head > 0)
        def _():
            loop(0, n, lambda step: send_out_to(head - 1, partner(step)))

        def one_device(step):
            other = partner(step)
            block = rows(other)
            out = attend(
                held[head, 0, block],
                held[head, 3, block],
                held[head, 1],
                held[head, 4],
                held[head, 2],
                held[head, 5],
            )
            for i in range(2):
                done[i, head, block] = out[i]
            pl.when(head == heads - 1)(lambda: send_out_to(head, other))

        loop(0, n, one_device)

    loop(0, heads, one_head)
    wide = (n - 1) * heads * E
    for i in range(2):
        wait_for(results[i].at[:, pl.ds(0, heads * E)], own_out.at[i])
        wait_for(results[i].at[:, pl.ds(0, wide)], recv_out.at[i])
    wait_for(done.at[:, :, pl.ds(0, far)], send_out)
    wait_for(held.at[:, :, pl.ds(0, far)], send_in)


def hand_over(one, two, out_one, out_two, sems):
    copies = [
        pltpu.make_async_copy(one, out_one, sems.at[0]),
        pltpu.make_async_copy(two, out_two, sems.at[1]),
    ]
    for copy in copies:
        copy.start()
    for copy in copies:
        copy.wait()


def per_device(n, *arrays):
    tokens, width = arrays[0].shape
    heads = width // E // n
    length = tokens * n
    shape = jax.ShapeDtypeStruct((tokens, width), jnp.bfloat16)
    both = pl.pallas_call(
        functools.partial(kernel, n, heads),
        out_shape=(pltpu.VMEM((tokens, width), jnp.bfloat16),) * 2,
        in_specs=[pl.BlockSpec(memory_space=pltpu.HBM)] * 6,
        out_specs=[pl.BlockSpec(memory_space=pl.ANY)] * 2,
        scratch_shapes=[
            pltpu.VMEM((heads, 6, length, E), jnp.bfloat16),
            pltpu.VMEM((2, heads, length, E), jnp.bfloat16),
            pltpu.SemaphoreType.REGULAR((n,)),
            pltpu.SemaphoreType.DMA,
            pltpu.SemaphoreType.DMA((heads,)),
            pltpu.SemaphoreType.DMA((heads,)),
            pltpu.SemaphoreType.DMA,
            pltpu.SemaphoreType.DMA((2,)),
            pltpu.SemaphoreType.DMA((2,)),
        ],
        compiler_params=pltpu.CompilerParams(
            collective_id=0, has_side_effects=True, vmem_limit_bytes=58 * 1024 * 1024
        ),
    )(*arrays)
    return pl.pallas_call(
        hand_over,
        out_shape=(shape, shape),
        in_specs=[pl.BlockSpec(memory_space=pl.ANY)] * 2,
        out_specs=[pl.BlockSpec(memory_space=pl.ANY)] * 2,
        scratch_shapes=[pltpu.SemaphoreType.DMA((2,))],
    )(*(pltpu.with_memory_space_constraint(one, pltpu.VMEM) for one in both))


def solution(mesh):
    spec = P(("clip", "seq"), None)
    return jax.shard_map(
        functools.partial(per_device, mesh.shape["seq"]),
        mesh=mesh,
        in_specs=(spec,) * 6,
        out_specs=(spec,) * 2,
        check_vma=False,
    )
```

time: 218 us -> 213 us (0.977); the launches traced: 215 us -> 213 us
  local copies, waits for them, and re-layouts: 3.47 us -> 0 us
    unnamed x4 -> x0, local copies, waits for them, and re-layouts: 3.47 us -> none
    pallas_call x1 -> x2, Pallas kernels: 211 us -> 212 us  [the longest x1 211 us: per_device(): pl.pallas_call(functools.partial(kernel, n, heads), out_shape=(pltpu.VMEM...]
where the time goes in v2:
time: 213 us
  Pallas kernels  212 us (100%)
    pallas_call x1, Pallas kernels, per_device(): pl.pallas_call(functools.partial(kernel, n, heads), out_shape=(pltpu.VMEM...  211 us

profile of v2, /device:TPU:33, one launch (start us, length us, event | category | flops | bytes accessed | tf_op | source)
XLA Modules:
  0.0 212.8 jit_solution(14276252955338897967)
XLA Ops:
  0.6 210.7 %shard_map.77 = (bf16[192,3072]{1,0:T(8,128)(2,1)S(1)}, bf16[192,3072]{1,0:T(8,128)(2,1)S(1)}) custom-call(bf16[192,3072]{1,0:T(8,128)(2,1)} %refs_0_.1, bf16[192,3072]{1,0:T(8,128)(2,1)} %refs_1_.1, bf16[192,3072]{1,0:T(8,128)(2,1)} %refs_2_.1, bf16[192,3072]{1,0:T(8,128)(2,1)} %refs_3_.1, bf16[192,3072]{1,0:T(8,128)(2,1)} %refs_4_.1, bf16[192,3072]{1,0:T(8,128)(2,1)} %refs_5_.1), custom_call_target="tpu_custom_call" | custom-call | tf_op jit(solution)/shard_map/pallas_call | solution.py:202
  211.4 1.4 shard_map.78

commit v3 on v2

--- a/solution.py
+++ b/solution.py
@@ -153,7 +153,7 @@
         def _():
             send_head(head + 2)
 
-        @pl.when(head > 0)
+        @pl.when(head > 1)
         def _():
             loop(0, n, lambda step: send_out_to(head - 1, partner(step)))
 
@@ -170,7 +170,7 @@
             )
             for i in range(2):
                 done[i, head, block] = out[i]
-            pl.when(head == heads - 1)(lambda: send_out_to(head, other))
+            pl.when((head == heads - 1) | (head == 0))(lambda: send_out_to(head, other))
 
         loop(0, n, one_device)
 

time: 213 us -> 213 us (level)
  no operation moved by 1% of the time
where the time goes in v3:
time: 213 us
  Pallas kernels  212 us (100%)
    pallas_call x1, Pallas kernels, per_device(): pl.pallas_call(functools.partial(kernel, n, heads), out_shape=(pltpu.VMEM...  211 us

profile of v3, /device:TPU:33, one launch (start us, length us, event | category | flops | bytes accessed | tf_op | source)
XLA Modules:
  0.0 212.8 jit_solution(12224753583185227836)
XLA Ops:
  0.6 210.8 %shard_map.77 = (bf16[192,3072]{1,0:T(8,128)(2,1)S(1)}, bf16[192,3072]{1,0:T(8,128)(2,1)S(1)}) custom-call(bf16[192,3072]{1,0:T(8,128)(2,1)} %refs_0_.1, bf16[192,3072]{1,0:T(8,128)(2,1)} %refs_1_.1, bf16[192,3072]{1,0:T(8,128)(2,1)} %refs_2_.1, bf16[192,3072]{1,0:T(8,128)(2,1)} %refs_3_.1, bf16[192,3072]{1,0:T(8,128)(2,1)} %refs_4_.1, bf16[192,3072]{1,0:T(8,128)(2,1)} %refs_5_.1), custom_call_target="tpu_custom_call" | custom-call | tf_op jit(solution)/shard_map/pallas_call | solution.py:202
  211.4 1.4 shard_map.78
